TPU v7x, 512 devices: a whole 4x8x8 slice. The times are simulated.
512 devices in a mesh: rad: 32 (over x_lo, y, core), ord: 16 (over z, x_hi).
Axes of the slice: x: 4 (x_hi: 2, x_lo: 2; x = x_hi * 2 + x_lo), y: 8, z: 8, core: 2. Of those that a mesh axis runs over, the one named last changes fastest.
Arguments:
- velocity: bfloat16 [6, 32, 133120], P(None, 'rad', 'ord'), may hold values from -0.5 to 0.5
- magnetic: bfloat16 [6, 32, 133120], P(None, 'rad', 'ord'), may hold values from -0.5 to 0.5
- legendre: bfloat16 [192, 133120], P('rad', 'ord'), may hold values from -1 to 1
- quad_weights: float32 [384], replicated, may hold values from 0.2 to 1.5
- orders: int32 [512], replicated, may hold values from 0 to 511, as said below
- offsets: int32 [512], P('ord'), may hold values from 0 to 8207, as said below
Outputs:
- motional: bfloat16 [6, 32, 133120], P(None, 'rad', 'ord')
- advected: bfloat16 [6, 32, 133120], P(None, 'rad', 'ord')
Inputs may be any that keep to these rules, and one draw needn't show every extreme that they name: Every order appears in exactly one slot; the 32 slots of one ord index hold orders m and 511 - m in pairs. Within one ord index, slot s owns packed entries offsets[s] to offsets[s] + 512 - orders[s] - 1; these runs do not intersect, fill entries 0 to 8207 exactly, and the shortest run of each ord index comes last.
All inputs are finite; a program needn't handle non-finite values.
Results may differ from a plain program's by a relative error of at most 0.0081.
Values may be sent and summed in bfloat16 or wider, within the bound.
No kernel may reach another device: no remote copies, remote signals or barrier semaphores. Data moves between devices by JAX's collectives and lax.ppermute only.
A program may use at most 64 MiB of HBM per device.

v0:
```python
import math

import jax
import jax.numpy as jnp
from jax import lax
from jax.sharding import PartitionSpec as P

L = 512
NTH_HALF = 192
NPHI = 1536


def extended(block, sides, width):
    for axis, dim in sides:
        count = lax.axis_size(axis)
        forward = [(i, i + 1) for i in range(count - 1)]
        backward = [(target, source) for source, target in forward]
        low = lax.ppermute(
            lax.slice_in_dim(block, block.shape[dim] - width, None, axis=dim), axis, forward
        )
        high = lax.ppermute(lax.slice_in_dim(block, 0, width, axis=dim), axis, backward)
        block = jnp.concatenate([low, block, high], axis=dim)
    return block


def wave_tables(orders, nphi):
    azimuth = jnp.arange(nphi, dtype=jnp.int32)
    phase_steps = orders[:, None] * azimuth[None, :] % nphi
    angles = phase_steps.astype(jnp.float32) * (2.0 * math.pi / nphi)
    factor = jnp.where(orders == 0, 1.0, 2.0).astype(jnp.float32)[:, None]
    inverse = jnp.stack([factor * jnp.cos(angles), -factor * jnp.sin(angles)], 1).astype(
        jnp.bfloat16
    )
    norm_scale = nphi ** (-0.5)
    forward = jnp.stack([norm_scale * jnp.cos(angles), -norm_scale * jnp.sin(angles)], 2)
    forward = jnp.transpose(forward, (1, 0, 2)).astype(jnp.bfloat16)
    return (inverse, forward)


def shards(velocity, magnetic, legendre, quad_weights, orders, offsets):
    slot_count = offsets.shape[0]
    packed_len = velocity.shape[2]
    shells = velocity.shape[1]
    ord_index = lax.axis_index("ord")
    local_orders = lax.dynamic_slice_in_dim(orders, ord_index * slot_count, slot_count)
    rimmed = extended(magnetic, (("rad", 1),), 1)
    dmag = ((rimmed[:, 2:].astype(jnp.float32) - rimmed[:, :-2].astype(jnp.float32)) * 0.5).astype(
        jnp.bfloat16
    )
    spectral = jnp.concatenate([velocity, magnetic, dmag], 0)
    spectral_pad = jnp.pad(jnp.transpose(spectral, (2, 1, 0)), ((0, L), (0, 0), (0, 0)))
    degree = jnp.arange(L, dtype=jnp.int32)
    positions = offsets[:, None] + degree[None, :]
    inside_run = degree[None, :] < (L - local_orders)[:, None]
    parity = jnp.where(degree % 2 == 0, 1.0, -1.0).astype(jnp.float32)
    dense_coef = jnp.where(
        inside_run[:, :, None, None], spectral_pad[positions], jnp.zeros((), jnp.bfloat16)
    )
    signed_pair = jnp.stack(
        [dense_coef, dense_coef * parity.astype(jnp.bfloat16)[None, :, None, None]], 3
    )
    signed_pair = signed_pair.reshape(slot_count, L, shells * 36)
    full_table = lax.all_gather(legendre, "rad", axis=0, tiled=True)
    padded_table = jnp.pad(full_table, ((0, 0), (0, L)))
    shared_tiles = jax.vmap(lambda first: lax.dynamic_slice_in_dim(padded_table, first, L, 1))(
        offsets
    )
    grid = jnp.einsum(
        "stj,sjc->stc", shared_tiles, signed_pair, preferred_element_type=jnp.float32
    ).astype(jnp.bfloat16)
    grid = grid.reshape(slot_count, NTH_HALF, shells, 36)
    inverse, forward = wave_tables(orders, NPHI)
    band_rows = NTH_HALF // lax.axis_size("ord")
    north_weight = lax.dynamic_slice_in_dim(quad_weights, ord_index * band_rows, band_rows)
    south_weight = lax.dynamic_slice_in_dim(quad_weights[::-1], ord_index * band_rows, band_rows)
    weights = jnp.stack([north_weight, south_weight], 1)
    column_block = lax.all_to_all(grid, "ord", split_axis=1, concat_axis=0, tiled=True)
    slot_total, theta_rows, item_count = column_block.shape[:3]
    columns = column_block.reshape(slot_total, theta_rows, item_count, 2, 3, 3, 2)
    physical = jnp.einsum(
        "stnhfcr,srp->fchtnp", columns, inverse, preferred_element_type=jnp.float32
    )
    flow_grid = physical[0]
    field_grid = physical[1]
    slope_grid = physical[2]
    motional = jnp.stack(
        [
            flow_grid[1] * field_grid[2] - flow_grid[2] * field_grid[1],
            flow_grid[2] * field_grid[0] - flow_grid[0] * field_grid[2],
            flow_grid[0] * field_grid[1] - flow_grid[1] * field_grid[0],
        ],
        0,
    )
    advected = flow_grid[0][None] * slope_grid
    products = jnp.concatenate([motional, advected], 0).astype(jnp.bfloat16)
    harmonic = jnp.einsum(
        "khtnp,psr->stnhkr", products, forward, preferred_element_type=jnp.float32
    )
    harmonic = (harmonic * weights[None, :, None, :, None, None]).astype(jnp.bfloat16)
    spread = harmonic.reshape(slot_total, theta_rows, item_count, 24)
    spectra = lax.all_to_all(spread, "ord", split_axis=0, concat_axis=1, tiled=True)
    column_block = spectra
    summed = jnp.einsum(
        "stj,stnq->sjnq", shared_tiles, column_block, preferred_element_type=jnp.float32
    )
    summed = summed.reshape(slot_count, L, shells, 2, 12)
    merged = summed[:, :, :, 0] + parity[None, :, None, None] * summed[:, :, :, 1]
    merged = jnp.where(inside_run[:, :, None, None], merged, 0.0).astype(jnp.bfloat16)
    targets = jnp.where(inside_run, positions, packed_len + L)
    packed = jnp.zeros((packed_len, shells, 12), jnp.bfloat16).at[targets].set(merged, mode="drop")
    result = jnp.transpose(packed, (2, 1, 0))
    return (result[:6], result[6:])


def solution(mesh):
    return jax.shard_map(
        shards,
        mesh=mesh,
        in_specs=(
            P(None, "rad", "ord"),
            P(None, "rad", "ord"),
            P("rad", "ord"),
            P(),
            P(),
            P("ord"),
        ),
        out_specs=(P(None, "rad", "ord"), P(None, "rad", "ord")),
        check_vma=False,
    )
```

profile of v0, /device:TPU:24, one launch (start us, length us, event | category | flops | bytes accessed | tf_op | source)
XLA Modules:
  0.0 354.5 jit_solution(11083150354328333113)
XLA Ops:
  7.2 2.1 collective-permute-start.1
  9.3 3.6 %collective-permute-start = (bf16[6,1,8320]{2,0,1:T(8,128)(2,1)}, bf16[6,1,8320]{2,0,1:T(8,128)(2,1)S(1)}, u32[]{:S(2)}, u32[]{:S(2)}) collective-permute-start(bf16[6,1,8320]{2,0,1:T(8,128)(2,1)} %param.7), channel_id=1, source_target_pairs={{16,0},{32,16},{48,32},{64,48},{80,64},{96,80},{112,96},{128,112},... | collective-permute-start | bytes 299528 | tf_op jit(solution)/shard_map/ppermute | solution.py:21
  16.1 15.3 %multiply_convert_fusion.3 = (bf16[512,1536,1]{0,1,2:T(8,128)(2,1)}, bf16[512,1536,1]{0,1,2:T(8,128)(2,1)}) fusion(s32[512]{0:T(512)} %param.10), kind=kLoop, calls=%fused_computation.24 | loop fusion | flops 10223616 | bytes 3147776 | tf_op jit(solution)/shard_map/convert.9
  32.4 2.1 copy.50
  34.5 1.8 pad_bitcast_fusion
  36.3 57.8 %gather_fusion = bf16[16384,18]{1,0:T(8,128)(2,1)} fusion(bf16[8832,18]{1,0:T(8,128)(2,1)S(1)} %pad_bitcast_fusion, s32[16384]{0:T(1024)S(1)} %broadcast_clamp_fusion), kind=kCustom, calls=%fused_computation | custom fusion | bytes 1245184 | tf_op jit(solution)/shard_map/gather | solution.py:57
  94.2 3.8 %copy.51 = bf16[32,512,1,1,18]{1,0,4,3,2:T(8,128)(2,1)S(1)} copy(bf16[32,512,1,1,18]{4,1,0,3,2:T(8,128)(2,1)} %bitcast.190) | data formatting | bytes 1179648 | tf_op jit(solution)/shard_map/gather | solution.py:57
  99.2 3.5 reshape.695
  102.6 2.0 pad.9
  104.6 95.6 %while.1 = (s32[]{:T(128)}, bf16[192,8832]{1,0:T(8,128)(2,1)}, s32[32,2]{0,1:T(2,128)S(1)}, bf16[32,192,512]{2,1,0:T(8,128)(2,1)}, s32[]{:T(128)}) while((s32[]{:T(128)}, bf16[192,8832]{1,0:T(8,128)(2,1)}, s32[32,2]{0,1:T(2,128)S(1)}, bf16[32,192,512]{2,1,0:T(8,128)(2,1)}, s32[]{:T(128)}) %tuple.31), condition=%wide.while_cond, body=%wide.while_body.sunk | while | flops 2 | bytes 393829 | solution.py:65
  105.2 2.4 bitcast_dynamic-update-slice_fusion.2
  108.2 2.4 bitcast_dynamic-update-slice_fusion.2
  111.2 2.4 bitcast_dynamic-update-slice_fusion.2
  114.2 2.4 bitcast_dynamic-update-slice_fusion.2
  117.2 2.4 bitcast_dynamic-update-slice_fusion.2
  120.2 2.4 bitcast_dynamic-update-slice_fusion.2
  123.2 2.4 bitcast_dynamic-update-slice_fusion.2
  126.1 2.4 bitcast_dynamic-update-slice_fusion.2
  129.1 2.4 bitcast_dynamic-update-slice_fusion.2
  132.1 2.4 bitcast_dynamic-update-slice_fusion.2
  135.1 2.4 bitcast_dynamic-update-slice_fusion.2
  138.1 2.4 bitcast_dynamic-update-slice_fusion.2
  141.1 2.4 bitcast_dynamic-update-slice_fusion.2
  144.0 2.4 bitcast_dynamic-update-slice_fusion.2
  147.0 2.4 bitcast_dynamic-update-slice_fusion.2
  150.0 2.4 bitcast_dynamic-update-slice_fusion.2
  153.0 2.4 bitcast_dynamic-update-slice_fusion.2
  156.0 2.4 bitcast_dynamic-update-slice_fusion.2
  159.0 2.4 bitcast_dynamic-update-slice_fusion.2
  162.0 2.4 bitcast_dynamic-update-slice_fusion.2
  165.0 2.4 bitcast_dynamic-update-slice_fusion.2
  168.0 2.4 bitcast_dynamic-update-slice_fusion.2
  170.9 2.4 bitcast_dynamic-update-slice_fusion.2
  173.9 2.4 bitcast_dynamic-update-slice_fusion.2
  176.9 2.4 bitcast_dynamic-update-slice_fusion.2
  179.9 2.4 bitcast_dynamic-update-slice_fusion.2
  182.9 2.4 bitcast_dynamic-update-slice_fusion.2
  185.9 2.4 bitcast_dynamic-update-slice_fusion.2
  188.9 2.4 bitcast_dynamic-update-slice_fusion.2
  191.9 2.4 bitcast_dynamic-update-slice_fusion.2
  194.9 2.4 bitcast_dynamic-update-slice_fusion.2
  197.9 2.4 bitcast_dynamic-update-slice_fusion.2
  200.3 5.2 %fusion.20 = bf16[32,192,1,36]{1,3,0,2:T(8,128)(2,1)S(1)} fusion(bf16[32,192,512]{2,1,0:T(8,128)(2,1)} %get-tuple-element.9, bf16[32,512,36]{1,0,2:T(8,128)(2,1)} %bitcast.200), kind=kOutput, calls=%fused_computation.36 | convolution fusion | flops 226713600 | bytes 7913472 | tf_op jit(solution)/shard_map/stj,sjc->stc/dot_general | solution.py:68
  205.5 1.5 copy.53
  207.0 4.7 %reshape.703 = bf16[16,2,6912]{2,1,0:T(2,128)(2,1)} reshape(bf16[192,1,32,36]{3,2,1,0:T(8,128)(2,1)S(1)} %bitcast.196) | data formatting | bytes 884736
  211.7 12.9 %all-to-all-start = ((bf16[16,2,6912]{2,1,0:T(2,128)(2,1)}), bf16[16,2,6912]{2,1,0:T(2,128)(2,1)S(1)}, u32[]{:S(2)}, u32[]{:S(2)}) async-start(bf16[16,2,6912]{2,1,0:T(2,128)(2,1)} %reshape.703), calls=%async_computation | async-start | bytes 884736 | tf_op jit(solution)/shard_map/all_to_all | solution.py:77
  224.6 15.3 %multiply_convert_fusion.1 = (bf16[512,1,1536]{2,0,1:T(8,128)(2,1)}, bf16[512,1,1536]{2,0,1:T(8,128)(2,1)}) fusion(s32[512]{0:T(512)S(1)} %copy-done.5, f32[512]{0:T(512)S(1)} %get-tuple-element.31, f32[512]{0:T(512)S(1)} %get-tuple-element.32), kind=kLoop, calls=%fused_computation.19 | loop fusion | flops 10223616 | bytes 3151872 | tf_op jit(solution)/shard_map/convert.7
  239.9 2.7 all-to-all-done
  242.6 4.5 %reshape.704 = bf16[192,1,32,36]{3,2,1,0:T(8,128)(2,1)S(1)} reshape(bf16[16,2,6912]{2,1,0:T(2,128)(2,1)S(1)} %all-to-all-done) | data formatting | bytes 884736
  247.1 3.6 %copy.77 = bf16[16,32,12,1,36]{1,0,2,4,3:T(8,128)(2,1)S(1)} copy(bf16[16,32,12,1,36]{4,1,2,0,3:T(8,128)(2,1)S(1)} %bitcast.195) | data formatting | bytes 884736 | tf_op jit(solution)/shard_map/reshape.4
  250.8 1.7 reshape.700
  252.5 3.1 fusion.16
  257.1 2.0 copy.66
  259.0 2.7 reshape.705
  261.7 6.9 %all-to-all-start.1 = ((bf16[16,2,4608]{2,1,0:T(2,128)(2,1)}), bf16[16,2,4608]{2,1,0:T(2,128)(2,1)S(1)}, u32[]{:S(2)}, u32[]{:S(2)}) async-start(bf16[16,2,4608]{2,1,0:T(2,128)(2,1)} %reshape.705), calls=%async_computation.1 | async-start | bytes 589824 | tf_op jit(solution)/shard_map/all_to_all | solution.py:101
  268.7 15.2 %all-to-all-done.1 = bf16[16,2,4608]{2,1,0:T(2,128)(2,1)S(1)} async-done(((bf16[16,2,4608]{2,1,0:T(2,128)(2,1)}), bf16[16,2,4608]{2,1,0:T(2,128)(2,1)S(1)}, u32[]{:S(2)}, u32[]{:S(2)}) %all-to-all-start.1) | async-done | bytes 294944 | tf_op jit(solution)/shard_map/all_to_all | solution.py:101
  283.9 2.4 reshape.706
  286.3 2.6 copy.78
  290.1 3.7 %fusion.54 = f32[32,512,24]{1,2,0:T(8,128)S(1)} fusion(bf16[32,192,512]{2,1,0:T(8,128)(2,1)} %get-tuple-element.9, bf16[32,192,24]{1,2,0:T(8,128)(2,1)S(1)} %copy.69), kind=kOutput, calls=%fused_computation.100 | convolution fusion | flops 150994944 | bytes 8159232 | tf_op jit(solution)/shard_map/stj,stnq->sjnq/dot_general | solution.py:103
  294.9 3.3 copy.79
  298.2 42.1 %scatter_custom_fusion = bf16[8320,12]{1,0:T(8,128)(2,1)S(1)} fusion(s32[16384]{0:T(1024)S(1)} %bitcast.203, bf16[16384,12]{1,0:T(8,128)(2,1)} %bitcast.199, bf16[]{:T(256)} %constant.20.clone.1), kind=kCustom, calls=%fused_computation.39 | custom fusion | bytes 200192 | tf_op jit(solution)/shard_map/scatter | solution.py:110
  340.4 2.4 fusion.53
  342.8 2.8 copy.72
  345.6 2.0 copy.73
  (110 shorter events, 27.8 us)
Async XLA Ops:
  7.2 25.0 %copy-start.3 = (bf16[6,1,8320]{2,0,1:T(8,128)(2,1)S(1)}, bf16[6,1,8320]{2,0,1:T(8,128)(2,1)}, u32[]{:S(2)}) copy-start(bf16[6,1,8320]{2,0,1:T(8,128)(2,1)} %param.7) | copy-start | bytes 299524
  7.2 25.0 %copy-start.4 = (bf16[6,1,8320]{2,0,1:T(8,128)(2,1)S(1)}, bf16[6,1,8320]{2,0,1:T(8,128)(2,1)}, u32[]{:S(2)}) copy-start(bf16[6,1,8320]{2,0,1:T(8,128)(2,1)} %param.6) | copy-start | bytes 299524
  7.2 92.0 %all-gather.3.cloned.1.call-start = ((), (), s32[]{:S(2)}) async-start(), calls=%async_computation.2 | async-start | bytes 4392960 | tf_op jit(solution)/shard_map/all_gather | solution.py:63
  7.2 24.9 %collective-permute-start.1 = (bf16[6,1,8320]{2,0,1:T(8,128)(2,1)}, bf16[6,1,8320]{2,0,1:T(8,128)(2,1)S(1)}, u32[]{:S(2)}, u32[]{:S(2)}) collective-permute-start(bf16[6,1,8320]{2,0,1:T(8,128)(2,1)} %param.7), channel_id=1, source_target_pairs={{0,16},{16,32},{32,48},{48,64},{64,80},{80,96},{96,112},{112,128},... | collective-permute-start | bytes 299528 | tf_op jit(solution)/shard_map/ppermute | solution.py:18
  9.3 22.9 %collective-permute-start = (bf16[6,1,8320]{2,0,1:T(8,128)(2,1)}, bf16[6,1,8320]{2,0,1:T(8,128)(2,1)S(1)}, u32[]{:S(2)}, u32[]{:S(2)}) collective-permute-start(bf16[6,1,8320]{2,0,1:T(8,128)(2,1)} %param.7), channel_id=1, source_target_pairs={{16,0},{32,16},{48,32},{64,48},{80,64},{96,80},{112,96},{128,112},... | collective-permute-start | bytes 299528 | tf_op jit(solution)/shard_map/ppermute | solution.py:21
  205.5 19.1 %copy-start.5 = (s32[512]{0:T(512)S(1)}, s32[512]{0:T(512)}, u32[]{:S(2)}) copy-start(s32[512]{0:T(512)} %param.10) | copy-start | bytes 6148
  211.7 31.0 %all-to-all-start = ((bf16[16,2,6912]{2,1,0:T(2,128)(2,1)}), bf16[16,2,6912]{2,1,0:T(2,128)(2,1)S(1)}, u32[]{:S(2)}, u32[]{:S(2)}) async-start(bf16[16,2,6912]{2,1,0:T(2,128)(2,1)} %reshape.703), calls=%async_computation | async-start | bytes 884736 | tf_op jit(solution)/shard_map/all_to_all | solution.py:77
  252.5 3.3 copy-start.1
  252.5 3.3 copy-start.2
  261.7 22.2 %all-to-all-start.1 = ((bf16[16,2,4608]{2,1,0:T(2,128)(2,1)}), bf16[16,2,4608]{2,1,0:T(2,128)(2,1)S(1)}, u32[]{:S(2)}, u32[]{:S(2)}) async-start(bf16[16,2,4608]{2,1,0:T(2,128)(2,1)} %reshape.705), calls=%async_computation.1 | async-start | bytes 589824 | tf_op jit(solution)/shard_map/all_to_all | solution.py:101
  342.8 2.8 copy-start
Sparse Core Ops, SparseCore 0:
  13.1 73.6 all-gather.2
where the time goes:
time: 356 us; the launch traced here: 354 us
  local copies, waits for them, and re-layouts  249 us (70%)
  other arithmetic  34.6 us (10%)
  starting transfers between devices  25.5 us (7%)
  waiting for transfers between devices  18 us (5%)
  between operations  14.4 us (4%)
  matrix products  12.8 us (4%)
    gather x96, local copies, waits for them, and re-layouts  95.6 us
    gather x2, local copies, waits for them, and re-layouts, shards(): spectral_pad[positions]  61.6 us
    scatter x1, local copies, waits for them, and re-layouts, shards(): jnp.zeros((packed_len, shells, 12), jnp.bfloat16).at[targets]  42.1 us
    another operation x3, other arithmetic  30.7 us
    unnamed x21, local copies, waits for them, and re-layouts  22.6 us
    all_to_all x1, waiting for transfers between devices, shards(): lax.all_to_all(spread, 'ord', split_axis=0, concat_axis=1, tiled=True)  15.2 us
    all_to_all x1, starting transfers between devices, shards(): lax.all_to_all(grid, 'ord', split_axis=1, concat_axis=0, tiled=True)  12.9 us
  transfers between devices with their start and end apart: 5, of which 2 were waited for; matrix products, arithmetic and copies ran while one was open for 29% of the time, Pallas kernels for 0%

commit v1 on v0

v1 whole, which is shorter than its diff:
```python
import math

import jax
import jax.numpy as jnp
import ml_dtypes
import numpy as np
from jax import lax
from jax.experimental import pallas as pl
from jax.experimental.pallas import tpu as pltpu
from jax.sharding import Mesh
from jax.sharding import PartitionSpec as P

L = 512
NTH_HALF = 192
NPHI = 1536
PACK = 8320
SLOTS = 32
WIN = 640
HALF = 4096
WIDE = PACK - HALF
RAD = ("xl", "y", "c")
ORD = ("z", "xh")
SWAP = ("xh", "z")
BANDS = 8
ROWS = 24
UNROLL = 32
VMEM_LIMIT = 24 * 1024 * 1024
F32 = jnp.float32
BF16 = jnp.bfloat16


def vmem():
    return pl.BlockSpec(memory_space=pltpu.VMEM)


def smem():
    return pl.BlockSpec(memory_space=pltpu.SMEM)


def anywhere():
    return pl.BlockSpec(memory_space=pl.ANY)


def params():
    return pltpu.CompilerParams(vmem_limit_bytes=VMEM_LIMIT)


def canonical_table():
    m = np.arange(L)[:, None]
    p = np.arange(NPHI)[None, :]
    angles = (m * p % NPHI).astype(np.float64) * (2.0 * math.pi / NPHI)
    factor = np.where(m == 0, 1.0, 2.0)
    table = np.concatenate([factor * np.cos(angles), -factor * np.sin(angles)], 0)
    return table.astype(np.float32).astype(ml_dtypes.bfloat16)


def band_rows(band):
    return (16 * band, 16 * band + 8, 128 + 8 * band, 192 + 8 * band)


def slot_window(off_ref, len_ref, s):
    start = off_ref[s]
    base = jnp.minimum((start // 128) * 128, PACK - WIN)
    base = pl.multiple_of(base, 128)
    return start, len_ref[s], base


def synthesis_kernel(off_ref, len_ref, spec_ref, same_ref, near_ref, far_ref, *refs):
    out_ref, coef_ref, acc_a, acc_b = refs
    lane = lax.broadcasted_iota(jnp.int32, (ROWS, WIN), 1)

    def mask_slot(s, carry):
        start, count, base = slot_window(off_ref, len_ref, s)
        degree = lane + (base - start)
        inside = (degree >= 0) & (degree < count)
        even = (degree & 1) == 0
        coef = jnp.where(inside, spec_ref[:, pl.ds(base, WIN)].astype(F32), 0.0)
        pair = jnp.concatenate([jnp.where(even, coef, 0.0), jnp.where(even, 0.0, coef)], 0)
        coef_ref[s] = pair.astype(BF16)
        return carry

    lax.fori_loop(0, SLOTS, mask_slot, 0, unroll=4)
    def one_slot(s, carry):
        start, count, base = slot_window(off_ref, len_ref, s)
        coef = coef_ref[s]
        both = jnp.concatenate(
            [
                lax.dot_general(
                    coef,
                    part[:, pl.ds(base, WIN)],
                    (((1,), (1,)), ((), ())),
                    preferred_element_type=F32,
                )
                for part in (same_ref, near_ref, far_ref)
            ],
            1,
        )
        north = both[:ROWS] + both[ROWS:]
        south = both[:ROWS] - both[ROWS:]
        acc_a[pl.ds(s, 24, stride=32), :] = north[:, 0:128]
        acc_b[pl.ds(s, 24, stride=32), :] = north[:, 128:256]
        acc_a[pl.ds(768 + s, 24, stride=32), :] = south[:, 0:128]
        acc_b[pl.ds(768 + s, 24, stride=32), :] = south[:, 128:256]
        return carry

    lax.fori_loop(0, SLOTS, one_slot, 0, unroll=UNROLL)
    for hemi in range(2):
        held = slice(768 * hemi, 768 * hemi + 640)
        turned = jnp.transpose(jnp.concatenate([acc_a[held], acc_b[held]], 1))
        for band in range(BANDS):
            rows = jnp.concatenate([turned[at : at + 6] for at in band_rows(band)], 0)
            out_ref[hemi * BANDS + band] = rows.astype(BF16)


def synthesis(offsets, lengths, spec, same, near, far):
    return pl.pallas_call(
        synthesis_kernel,
        out_shape=jax.ShapeDtypeStruct((16, ROWS, 640), BF16),
        in_specs=[smem(), smem(), vmem(), vmem(), vmem(), vmem()],
        out_specs=vmem(),
        scratch_shapes=[
            pltpu.VMEM((SLOTS, 2 * ROWS, WIN), BF16),
            pltpu.VMEM((1536, 128), F32),
            pltpu.VMEM((1536, 128), F32),
        ],
        compiler_params=params(),
        name="synthesis",
    )(offsets, lengths, spec, same, near, far)


def join_halves(first, second, half):
    low = lax.broadcasted_iota(jnp.int32, first.shape, 1) < 64
    if half == 0:
        return jnp.where(low, first, pltpu.roll(second, 64, 1))
    return jnp.where(low, pltpu.roll(first, 64, 1), second)


def waves_kernel(source_ref, table_ref, after_ref, out_ref):
    column = lax.broadcasted_iota(jnp.int32, (2 * L, 2 * L), 1)
    chosen = jnp.where(column == source_ref[...], 1.0, 0.0).astype(BF16)
    step = 512
    for at in range(0, NPHI, step):
        out_ref[:, at : at + step] = jnp.dot(
            chosen, table_ref[:, at : at + step], preferred_element_type=F32
        ).astype(BF16)


def wave_rows(source, table, after):
    return pl.pallas_call(
        waves_kernel,
        out_shape=jax.ShapeDtypeStruct((2 * L, NPHI), BF16),
        in_specs=[vmem(), vmem(), anywhere()],
        out_specs=vmem(),
        compiler_params=params(),
        cost_estimate=pl.CostEstimate(
            flops=8 * L * L * NPHI, bytes_accessed=8 * L * NPHI, transcendentals=0
        ),
        name="waves",
    )(source, table, after)


def azimuth_kernel(g_ref, t_ref, row_ref, lane_ref, out_ref, a_ref, h_ref):
    for c in range(9):
        tile = slice(128 * (c // 2), 128 * (c // 2) + 128)
        for pair in range(8):
            first = g_ref[2 * pair][:, tile].astype(F32)
            second = g_ref[2 * pair + 1][:, tile].astype(F32)
            a_ref[ROWS * c : ROWS * (c + 1), 128 * pair : 128 * (pair + 1)] = join_halves(
                first, second, c % 2
            )
    values = a_ref[...].astype(BF16)
    step = 512
    for chunk in range(NPHI // step):
        waves = t_ref[:, step * chunk : step * (chunk + 1)]
        grid = jnp.dot(values, waves, preferred_element_type=F32)
        u = [grid[ROWS * c : ROWS * (c + 1)] for c in range(3)]
        b = [grid[ROWS * (3 + c) : ROWS * (4 + c)] for c in range(3)]
        d = [grid[ROWS * (6 + c) : ROWS * (7 + c)] for c in range(3)]
        products = jnp.concatenate(
            [
                u[1] * b[2] - u[2] * b[1],
                u[2] * b[0] - u[0] * b[2],
                u[0] * b[1] - u[1] * b[0],
                u[0] * d[0],
                u[0] * d[1],
                u[0] * d[2],
            ],
            0,
        ).astype(BF16)
        part = lax.dot_general(
            products, waves, (((1,), (1,)), ((), ())), preferred_element_type=F32
        )
        if chunk == 0:
            h_ref[...] = part
        else:
            h_ref[...] += part
    h_ref[...] = h_ref[...] * row_ref[...] * lane_ref[...]
    for dest in range(16):
        tile = slice(128 * (dest // 2), 128 * (dest // 2) + 128)
        parts = []
        for k in range(0, 6, 2):
            first = h_ref[ROWS * k : ROWS * (k + 1), tile]
            second = h_ref[ROWS * (k + 1) : ROWS * (k + 2), tile]
            parts.append(join_halves(first, second, dest % 2))
        out_ref[dest] = jnp.concatenate(parts, 1).astype(BF16)


def azimuth(grid, waves, row_scale, lane_scale):
    return pl.pallas_call(
        azimuth_kernel,
        out_shape=jax.ShapeDtypeStruct((16, ROWS, 384), BF16),
        in_specs=[vmem()] * 4,
        out_specs=vmem(),
        scratch_shapes=[pltpu.VMEM((216, 1024), F32), pltpu.VMEM((144, 1024), F32)],
        compiler_params=params(),
        name="azimuth",
    )(grid, waves, row_scale, lane_scale)


def analysis_kernel(off_ref, len_ref, r_ref, same_ref, near_ref, far_ref, mot_ref, adv_ref, *refs):
    wide, turned_a, turned_b, out = refs
    gap = jnp.zeros((2, 384), F32)
    for hemi in range(2):
        for band in range(BANDS):
            held = r_ref[hemi * BANDS + band].astype(F32)
            for i, at in enumerate(band_rows(band)):
                wide[at : at + 8, :] = jnp.concatenate([held[6 * i : 6 * i + 6], gap], 0)
        flip = jnp.transpose(wide[...])
        at = 512 * hemi
        for turned, lanes in ((turned_a, slice(0, 128)), (turned_b, slice(128, 256))):
            turned[at : at + 192] = flip[0:192, lanes]
            turned[at + 192 : at + 256] = jnp.zeros((64, 128), F32)
            turned[at + 256 : at + 448] = flip[192:384, lanes]
            turned[at + 448 : at + 512] = jnp.zeros((64, 128), F32)
    out[...] = jnp.zeros_like(out)
    lane = lax.broadcasted_iota(jnp.int32, (16, WIN), 1)

    def one_slot(s, carry):
        start, count, base = slot_window(off_ref, len_ref, s)
        degree = lane + (base - start)
        inside = (degree >= 0) & (degree < count)
        even = (degree & 1) == 0
        rows_a = turned_a[pl.ds(s, 32, stride=32), :].astype(BF16)
        rows_b = turned_b[pl.ds(s, 32, stride=32), :].astype(BF16)
        window = pl.ds(base, WIN)
        both = jnp.dot(rows_a, same_ref[:, window], preferred_element_type=F32)
        rest = jnp.concatenate([near_ref[:, window], far_ref[:, window]], 0)
        both += jnp.dot(rows_b, rest, preferred_element_type=F32)
        merged = both[:16] + jnp.where(even, both[16:], -both[16:])
        held = out[:, pl.ds(base, WIN)]
        out[:, pl.ds(base, WIN)] = jnp.where(inside, merged, held)
        return carry

    lax.fori_loop(0, SLOTS, one_slot, 0, unroll=UNROLL)
    mot_ref[...] = out[0:6].astype(BF16)
    adv_ref[...] = out[8:14].astype(BF16)


def analysis(offsets, lengths, spectra, same, near, far):
    shape = jax.ShapeDtypeStruct((6, PACK), BF16)
    return pl.pallas_call(
        analysis_kernel,
        out_shape=(shape, shape),
        in_specs=[smem(), smem(), vmem(), vmem(), vmem(), vmem()],
        out_specs=(vmem(), vmem()),
        scratch_shapes=[
            pltpu.VMEM((256, 384), F32),
            pltpu.VMEM((1024, 128), F32),
            pltpu.VMEM((1024, 128), F32),
            pltpu.VMEM((16, PACK), F32),
        ],
        compiler_params=params(),
        name="analysis",
    )(offsets, lengths, spectra, same, near, far)


def entry_kernel(p_ref, padded_ref, p_out):
    rows = p_ref[...].astype(F32)
    padded_ref[...] = jnp.concatenate([rows, jnp.zeros((2, PACK), F32)], 0).astype(BF16)
    p_out[...] = p_ref[...]


def entry(legendre):
    return pl.pallas_call(
        entry_kernel,
        out_shape=(
            jax.ShapeDtypeStruct((8, PACK), BF16),
            jax.ShapeDtypeStruct((6, PACK), BF16),
        ),
        in_specs=[vmem()],
        out_specs=(vmem(),) * 2,
        compiler_params=params(),
        name="entry",
    )(legendre)


def hold_kernel(x_ref, after_ref, out_ref):
    out_ref[...] = x_ref[...]


def hold(x, after):
    return pl.pallas_call(
        hold_kernel,
        out_shape=jax.ShapeDtypeStruct(x.shape, x.dtype),
        in_specs=[vmem(), anywhere()],
        out_specs=vmem(),
        compiler_params=params(),
        name="hold",
    )(x, after)


def gathered_table(legendre):
    padded, legendre = entry(legendre)
    same = lax.all_gather(padded, ("y", "c"), axis=0, tiled=True)
    other = lax.ppermute(legendre, "xl", [(0, 1), (1, 0)])
    near = lax.all_gather(other, "y", axis=0)
    near = jnp.pad(near, ((0, 0), (0, 2), (0, 0))).reshape(64, PACK)
    far = lax.ppermute(near, "c", [(0, 1), (1, 0)])
    return same, near, far


def radial_slope(magnetic, after):
    count = lax.axis_size(RAD)
    links = [(i, i + 1) for i in range(1, count - 1, 2)]
    magnetic = hold(magnetic, after)
    swapped = lax.ppermute(magnetic, "c", [(0, 1), (1, 0)])
    linked = lax.ppermute(magnetic, RAD, links + [(j, i) for i, j in links])
    swapped, linked = swapped.astype(F32), linked.astype(F32)
    first = lax.axis_index("c") == 0
    slope = jnp.where(first, swapped - linked, linked - swapped)
    return (slope * 0.5).astype(BF16)


def table_weights(quad_weights):
    row = jnp.arange(6 * ROWS, dtype=jnp.int32) % ROWS
    run = row // 6
    column = lax.axis_index("xl")
    core = lax.axis_index("c")
    column = jnp.where(run < 2, column, 1 - column)
    core = jnp.where(run < 2, run, jnp.where(run == 2, core, 1 - core))
    theta = ((column * 8 + lax.axis_index("z")) * 2 + core) * 6 + row % 6
    theta = jnp.where(lax.axis_index("xh") == 0, theta, 2 * NTH_HALF - 1 - theta)
    chosen = theta[:, None] == jnp.arange(2 * NTH_HALF, dtype=jnp.int32)[None, :]
    return jnp.sum(jnp.where(chosen, quad_weights[None, :], 0.0), 1, keepdims=True)


def shards(velocity, magnetic, legendre, quad_weights, orders, offsets):
    velocity = velocity.reshape(6, PACK)
    magnetic = magnetic.reshape(6, PACK)
    ord_index = lax.axis_index(ORD)
    local_orders = lax.dynamic_slice_in_dim(orders, ord_index * SLOTS, SLOTS)
    lengths = L - local_orders
    same, near, far = gathered_table(legendre)
    slope = radial_slope(magnetic, near)
    spec = jnp.concatenate([velocity, magnetic, slope, jnp.zeros_like(velocity)], 0)

    swapped = jnp.transpose(orders.reshape(8, 2, SLOTS), (1, 0, 2)).reshape(L)
    source = swapped.reshape(16, 1, SLOTS) + jnp.array([0, L], jnp.int32)[None, :, None]
    unscale = jnp.where(swapped == 0, 1.0, 0.5).astype(F32).reshape(16, 1, SLOTS)
    lane_scale = jnp.broadcast_to(unscale, (16, 2, SLOTS)).reshape(1, 2 * L)
    row_scale = table_weights(quad_weights) * (NPHI ** (-0.5))
    grid = synthesis(offsets, lengths, spec, same, near, far)
    waves = wave_rows(source.reshape(2 * L, 1), jnp.asarray(canonical_table()), grid)
    grid = lax.all_to_all(grid, SWAP, 0, 0)
    harmonic = azimuth(grid, waves, row_scale, lane_scale)
    spectra = lax.all_to_all(harmonic, SWAP, 0, 0)
    motional, advected = analysis(offsets, lengths, spectra, same, near, far)
    return motional.reshape(6, 1, PACK), advected.reshape(6, 1, PACK)


def solution(mesh):
    fine = Mesh(mesh.devices.reshape(2, 8, 2, 8, 2), RAD + ORD)
    return jax.shard_map(
        shards,
        mesh=fine,
        in_specs=(
            P(None, RAD, ORD),
            P(None, RAD, ORD),
            P(RAD, ORD),
            P(),
            P(),
            P(ORD),
        ),
        out_specs=(P(None, RAD, ORD), P(None, RAD, ORD)),
        check_vma=False,
    )
```

time: 356 us -> 127 us (0.36)
  the two profiles are of different devices: /device:TPU:24 before, /device:TPU:2 now
where the time goes in v1:
time: 127 us
  blocking collectives  45 us (35%)
  starting transfers between devices  26.4 us (21%)
  Pallas kernels  16.4 us (13%)
  between operations  14.2 us (11%)
  waiting for transfers between devices  13 us (10%)
  local copies, waits for them, and re-layouts  10.4 us (8%)
  other arithmetic  1.33 us (1%)
    all_gather x1, blocking collectives, gathered_table(): near = lax.all_gather(other, 'y', axis=0)  28.3 us
    all_to_all x1, blocking collectives, shards(): spectra = lax.all_to_all(harmonic, SWAP, 0, 0)  16.8 us
    all_to_all x1, starting transfers between devices, shards(): grid = lax.all_to_all(grid, SWAP, 0, 0)  10.8 us
    unnamed x20, local copies, waits for them, and re-layouts  8.65 us
    all_to_all x1, waiting for transfers between devices, shards(): grid = lax.all_to_all(grid, SWAP, 0, 0)  8.58 us
    ppermute x1, starting transfers between devices, gathered_table(): other = lax.ppermute(legendre, 'xl', [(0, 1), (1, 0)])  7.8 us
    pallas_call x1, Pallas kernels, synthesis(): pl.pallas_call(synthesis_kernel, out_shape=jax.ShapeDtypeStruct((16, ROWS...  6.59 us
    ppermute x1, starting transfers between devices, radial_slope(): linked = lax.ppermute(magnetic, RAD, links + [(j, i) for i, j in links])  3.97 us
  transfers between devices with their start and end apart: 6, of which 4 were waited for; matrix products, arithmetic and copies ran while one was open for 2% of the time, Pallas kernels for 3%

profile of v1, /device:TPU:2, one launch (start us, length us, event | category | flops | bytes accessed | tf_op | source)
XLA Modules:
  0.0 126.8 jit_solution(9344120483821158300)
XLA Ops:
  7.2 0.0 all-gather.4.cloned.1.call-start
  7.2 0.0 copy-start.5
  7.2 0.9 copy-done.5
  8.1 0.7 entry.1
  8.8 7.8 %collective-permute-start = (bf16[6,8320]{1,0:T(8,128)(2,1)S(1)}, bf16[6,8320]{1,0:T(8,128)(2,1)S(1)}, u32[]{:S(2)}, u32[]{:S(2)}) collective-permute-start(bf16[6,8320]{1,0:T(8,128)(2,1)S(1)} %get-tuple-element.6), channel_id=1, source_target_pairs={{0,256},{256,0},{1,257},{257,1},{2,258},{258,2},{3,259},{259,3},{4... | collective-permute-start | bytes 299528 | tf_op jit(solution)/shard_map/ppermute | solution.py:315
  16.6 0.0 all-gather.4.cloned.1.call-update
  16.6 0.8 reshape.106
  17.4 0.1 broadcast_add_fusion
  17.5 0.1 pad.8.clone
  17.6 2.0 %collective-permute-done = bf16[6,8320]{1,0:T(8,128)(2,1)S(1)} collective-permute-done((bf16[6,8320]{1,0:T(8,128)(2,1)S(1)}, bf16[6,8320]{1,0:T(8,128)(2,1)S(1)}, u32[]{:S(2)}, u32[]{:S(2)}) %collective-permute-start) | collective-permute-done | bytes 99872 | tf_op jit(solution)/shard_map/ppermute | solution.py:315
  19.6 28.3 %all-gather.1 = bf16[8,6,8320]{2,1,0:T(8,128)(2,1)S(1)} all-gather(bf16[1,6,8320]{2,1,0:T(8,128)(2,1)S(1)} %bitcast.16), channel_id=2, replica_groups=mesh['xl'=2,'y'=8,'c'=2,'z'=8,'xh'=2] {'y'}, dimensions={0}, use_global_device_ids=true | all-gather | bytes 898560 | tf_op jit(solution)/shard_map/all_gather | solution.py:316
  47.8 0.0 copy-start.4
  47.8 0.2 pad_bitcast_fusion.after_ref.near_ref
  48.0 0.0 copy-start.8
  48.0 0.7 copy-done.4
  48.7 0.0 copy-start.6
  48.8 1.9 %collective-permute-start.1 = (bf16[6,8320]{1,0:T(8,128)(2,1)S(1)}, bf16[6,8320]{1,0:T(8,128)(2,1)S(1)}, u32[]{:S(2)}, u32[]{:S(2)}) collective-permute-start(bf16[6,8320]{1,0:T(8,128)(2,1)S(1)} %hold.1), channel_id=1, source_target_pairs={{0,16},{16,0},{1,17},{17,1},{2,18},{18,2},{3,19},{19,3},{4,20},{20... | collective-permute-start | bytes 299528 | tf_op jit(solution)/shard_map/ppermute | solution.py:326
  50.7 4.0 %collective-permute-start.2 = (bf16[6,8320]{1,0:T(8,128)(2,1)S(1)}, bf16[6,8320]{1,0:T(8,128)(2,1)S(1)}, u32[]{:S(2)}, u32[]{:S(2)}) collective-permute-start(bf16[6,8320]{1,0:T(8,128)(2,1)S(1)} %hold.1), channel_id=1, source_target_pairs={{16,32},{48,64},{80,96},{112,128},{144,160},{176,192},{208,224},{2... | collective-permute-start | bytes 299528 | tf_op jit(solution)/shard_map/ppermute | solution.py:327
  54.7 0.8 dynamic-slice_subtract_fusion.len_ref
  55.4 1.9 %collective-permute-start.3 = (bf16[64,8320]{1,0:T(8,128)(2,1)S(1)}, bf16[64,8320]{1,0:T(8,128)(2,1)S(1)}, u32[]{:S(2)}, u32[]{:S(2)}) collective-permute-start(bf16[64,8320]{1,0:T(8,128)(2,1)S(1)} %pad_bitcast_fusion.after_ref.near_ref), channel_id=1, source_target_pairs={{0,16},{16,0},{1,17},{17,1},{2,18},{18,2},{3,19},{19,3},{4,20},{20... | collective-permute-start | bytes 3194888 | tf_op jit(solution)/shard_map/ppermute | solution.py:318
  57.3 0.0 collective-permute-done.1
  57.4 1.9 %collective-permute-done.2 = bf16[6,8320]{1,0:T(8,128)(2,1)S(1)} collective-permute-done((bf16[6,8320]{1,0:T(8,128)(2,1)S(1)}, bf16[6,8320]{1,0:T(8,128)(2,1)S(1)}, u32[]{:S(2)}, u32[]{:S(2)}) %collective-permute-start.2) | collective-permute-done | bytes 99872 | tf_op jit(solution)/shard_map/ppermute | solution.py:327
  59.3 0.1 fusion.2
  59.3 0.0 copy-done.8
  59.4 0.2 maximum_maximum_fusion.spec_ref
  59.5 0.4 collective-permute-done.3.far_ref
  60.0 0.0 all-gather.4.cloned.1.call-done.same_ref
  60.0 0.0 copy-done.6
  60.0 0.0 copy-start
  60.0 1.6 %copy-done = bf16[128,8320]{1,0:T(8,128)(2,1)S(1)} copy-done((bf16[128,8320]{1,0:T(8,128)(2,1)S(1)}, bf16[128,8320]{1,0:T(8,128)(2,1)}, u32[]{:S(2)}) %copy-start) | copy-done | bytes 2129944
  61.6 6.6 %synthesis.1.after_ref = bf16[16,24,640]{2,1,0:T(8,128)(2,1)} custom-call(s32[32]{0:T(128)S(1)} %copy-done.6, s32[32]{0:T(128)S(1)} %dynamic-slice_subtract_fusion.len_ref, bf16[24,8320]{1,0:T(8,128)(2,1)S(1)} %maximum_maximum_fusion.spec_ref, bf16[128,8320]{1,0:T(8,128)(2,1)S(1)} %copy-done, bf16[64,8320]{1,0:T(8,128)(2,1)S(1)} %pad_bitcast_fusion.after_ref.near_ref, ...), custom_call_target="tpu_custom_call" | custom-call | tf_op jit(solution)/shard_map/synthesis/pallas_call | solution.py:116
  68.2 0.0 copy-start.9
  68.2 10.8 %all-to-all-start = ((bf16[16,24,640]{2,1,0:T(8,128)(2,1)}), bf16[16,24,640]{2,1,0:T(8,128)(2,1)S(1)}, u32[]{:S(2)}, u32[]{:S(2)}) async-start(bf16[16,24,640]{2,1,0:T(8,128)(2,1)} %synthesis.1.after_ref), calls=%async_computation | async-start | bytes 983040 | tf_op jit(solution)/shard_map/all_to_all | solution.py:364
  79.0 0.5 add.101.source_ref
  79.6 0.0 copy-done.9
  79.6 0.2 select_reduce_fusion
  79.8 0.1 copy.20.row_ref
  79.9 0.1 reshape.107.lane_ref
  80.0 0.0 copy-start.7
  80.0 1.9 %copy-done.7 = bf16[1024,1536]{1,0:T(8,128)(2,1)S(1)} copy-done((bf16[1024,1536]{1,0:T(8,128)(2,1)S(1)}, bf16[1024,1536]{1,0:T(8,128)(2,1)}, u32[]{:S(2)}) %copy-start.7) | copy-done | bytes 3145752
  81.9 3.4 %waves.1.t_ref = bf16[1024,1536]{1,0:T(8,128)(2,1)S(1)} custom-call(s32[1024,1]{1,0:T(8,128)S(1)} %add.101.source_ref, bf16[1024,1536]{1,0:T(8,128)(2,1)S(1)} %copy-done.7, bf16[16,24,640]{2,1,0:T(8,128)(2,1)} %synthesis.1.after_ref), custom_call_target="tpu_custom_call" | custom-call | flops 3221225472 | bytes 6291456 | tf_op jit(solution)/shard_map/waves/pallas_call | solution.py:149
  85.4 0.0 copy-start.2
  85.4 1.6 %copy-done.2 = bf16[1024,1536]{1,0:T(8,128)(2,1)} copy-done((bf16[1024,1536]{1,0:T(8,128)(2,1)}, bf16[1024,1536]{1,0:T(8,128)(2,1)S(1)}, u32[]{:S(2)}) %copy-start.2) | copy-done | bytes 3145752
  87.0 8.6 %all-to-all-done.g_ref = bf16[16,24,640]{2,1,0:T(8,128)(2,1)S(1)} async-done(((bf16[16,24,640]{2,1,0:T(8,128)(2,1)}), bf16[16,24,640]{2,1,0:T(8,128)(2,1)S(1)}, u32[]{:S(2)}, u32[]{:S(2)}) %all-to-all-start) | async-done | bytes 491552 | tf_op jit(solution)/shard_map/all_to_all | solution.py:364
  95.6 0.0 copy-start.3
  95.6 1.9 %copy-done.3 = bf16[1024,1536]{1,0:T(8,128)(2,1)S(1)} copy-done((bf16[1024,1536]{1,0:T(8,128)(2,1)S(1)}, bf16[1024,1536]{1,0:T(8,128)(2,1)}, u32[]{:S(2)}) %copy-start.3) | copy-done | bytes 3145752
  97.5 0.0 copy-start.1
  97.5 2.2 %azimuth.1 = bf16[16,24,384]{2,1,0:T(8,128)(2,1)S(1)} custom-call(bf16[16,24,640]{2,1,0:T(8,128)(2,1)S(1)} %all-to-all-done.g_ref, bf16[1024,1536]{1,0:T(8,128)(2,1)S(1)} %copy-done.3, f32[144,1]{1,0:T(8,128)S(1)} %copy.20.row_ref, f32[1,1024]{1,0:T(1,128)S(1)} %reshape.107.lane_ref), custom_call_target="tpu_custom_call" | custom-call | tf_op jit(solution)/shard_map/azimuth/pallas_call | solution.py:209
  99.7 16.8 %all_to_all.10.r_ref = bf16[16,24,384]{2,1,0:T(8,128)(2,1)S(1)} all-to-all(bf16[16,24,384]{2,1,0:T(8,128)(2,1)S(1)} %azimuth.1), channel_id=1, replica_groups=mesh['xl'=2,'y'=8,'c'=2,'z'=8,'xh'=2] {'xh','z'}, dimensions={0} | all-to-all | bytes 589824 | tf_op jit(solution)/shard_map/all_to_all | solution.py:366
  116.5 0.0 copy-done.1
  116.5 3.4 %analysis.1 = (bf16[6,8320]{1,0:T(8,128)(2,1)}, bf16[6,8320]{1,0:T(8,128)(2,1)}) custom-call(s32[32]{0:T(128)S(1)} %copy-done.6, s32[32]{0:T(128)S(1)} %dynamic-slice_subtract_fusion.len_ref, bf16[16,24,384]{2,1,0:T(8,128)(2,1)S(1)} %all_to_all.10.r_ref, bf16[128,8320]{1,0:T(8,128)(2,1)S(1)} %copy-done.1, ...), custom_call_target="tpu_custom_call" | custom-call | tf_op jit(solution)/shard_map/analysis/pallas_call | solution.py:261
  (8 shorter events, 0.1 us)
Async XLA Ops:
  7.2 52.8 %all-gather.4.cloned.1.call-start = ((), (), s32[]{:S(2)}) async-start(), calls=%async_computation.2 | async-start | bytes 2263040 | tf_op jit(solution)/shard_map/all_gather | solution.py:314
  7.2 0.9 copy-start.5
  8.8 10.8 %collective-permute-start = (bf16[6,8320]{1,0:T(8,128)(2,1)S(1)}, bf16[6,8320]{1,0:T(8,128)(2,1)S(1)}, u32[]{:S(2)}, u32[]{:S(2)}) collective-permute-start(bf16[6,8320]{1,0:T(8,128)(2,1)S(1)} %get-tuple-element.6), channel_id=1, source_target_pairs={{0,256},{256,0},{1,257},{257,1},{2,258},{258,2},{3,259},{259,3},{4... | collective-permute-start | bytes 299528 | tf_op jit(solution)/shard_map/ppermute | solution.py:315
  47.8 0.9 copy-start.4
  48.0 11.3 %copy-start.8 = (bf16[6,1,8320]{2,0,1:T(8,128)(2,1)S(1)}, bf16[6,1,8320]{2,0,1:T(8,128)(2,1)}, u32[]{:S(2)}) copy-start(bf16[6,1,8320]{2,0,1:T(8,128)(2,1)} %param.8) | copy-start | bytes 299524
  48.7 11.3 %copy-start.6 = (s32[32]{0:T(128)S(1)}, s32[32]{0:T(128)}, u32[]{:S(2)}) copy-start(s32[32]{0:T(128)} %off_ref.3) | copy-start | bytes 388
  48.8 8.6 %collective-permute-start.1 = (bf16[6,8320]{1,0:T(8,128)(2,1)S(1)}, bf16[6,8320]{1,0:T(8,128)(2,1)S(1)}, u32[]{:S(2)}, u32[]{:S(2)}) collective-permute-start(bf16[6,8320]{1,0:T(8,128)(2,1)S(1)} %hold.1), channel_id=1, source_target_pairs={{0,16},{16,0},{1,17},{17,1},{2,18},{18,2},{3,19},{19,3},{4,20},{20... | collective-permute-start | bytes 299528 | tf_op jit(solution)/shard_map/ppermute | solution.py:326
  50.7 8.6 %collective-permute-start.2 = (bf16[6,8320]{1,0:T(8,128)(2,1)S(1)}, bf16[6,8320]{1,0:T(8,128)(2,1)S(1)}, u32[]{:S(2)}, u32[]{:S(2)}) collective-permute-start(bf16[6,8320]{1,0:T(8,128)(2,1)S(1)} %hold.1), channel_id=1, source_target_pairs={{16,32},{48,64},{80,96},{112,128},{144,160},{176,192},{208,224},{2... | collective-permute-start | bytes 299528 | tf_op jit(solution)/shard_map/ppermute | solution.py:327
  55.4 4.6 %collective-permute-start.3 = (bf16[64,8320]{1,0:T(8,128)(2,1)S(1)}, bf16[64,8320]{1,0:T(8,128)(2,1)S(1)}, u32[]{:S(2)}, u32[]{:S(2)}) collective-permute-start(bf16[64,8320]{1,0:T(8,128)(2,1)S(1)} %pad_bitcast_fusion.after_ref.near_ref), channel_id=1, source_target_pairs={{0,16},{16,0},{1,17},{17,1},{2,18},{18,2},{3,19},{19,3},{4,20},{20... | collective-permute-start | bytes 3194888 | tf_op jit(solution)/shard_map/ppermute | solution.py:318
  60.0 1.6 %copy-start = (bf16[128,8320]{1,0:T(8,128)(2,1)S(1)}, bf16[128,8320]{1,0:T(8,128)(2,1)}, u32[]{:S(2)}) copy-start(bf16[128,8320]{1,0:T(8,128)(2,1)} %all-gather.4.cloned.1.call-done.same_ref) | copy-start | bytes 6389764
  68.2 11.4 %copy-start.9 = (f32[384]{0:T(512)S(1)}, f32[384]{0:T(512)}, u32[]{:S(2)}) copy-start(f32[384]{0:T(512)} %param.11) | copy-start | bytes 4612
  68.2 27.4 %all-to-all-start = ((bf16[16,24,640]{2,1,0:T(8,128)(2,1)}), bf16[16,24,640]{2,1,0:T(8,128)(2,1)S(1)}, u32[]{:S(2)}, u32[]{:S(2)}) async-start(bf16[16,24,640]{2,1,0:T(8,128)(2,1)} %synthesis.1.after_ref), calls=%async_computation | async-start | bytes 983040 | tf_op jit(solution)/shard_map/all_to_all | solution.py:364
  80.0 1.9 %copy-start.7 = (bf16[1024,1536]{1,0:T(8,128)(2,1)S(1)}, bf16[1024,1536]{1,0:T(8,128)(2,1)}, u32[]{:S(2)}) copy-start(bf16[1024,1536]{1,0:T(8,128)(2,1)} %constant.78.clone.table_ref) | copy-start | bytes 9437188
  85.4 1.6 %copy-start.2 = (bf16[1024,1536]{1,0:T(8,128)(2,1)}, bf16[1024,1536]{1,0:T(8,128)(2,1)S(1)}, u32[]{:S(2)}) copy-start(bf16[1024,1536]{1,0:T(8,128)(2,1)S(1)} %waves.1.t_ref) | copy-start | bytes 9437188
  95.6 1.9 %copy-start.3 = (bf16[1024,1536]{1,0:T(8,128)(2,1)S(1)}, bf16[1024,1536]{1,0:T(8,128)(2,1)}, u32[]{:S(2)}) copy-start(bf16[1024,1536]{1,0:T(8,128)(2,1)} %copy-done.2) | copy-start | bytes 9437188
  97.5 19.0 %copy-start.1 = (bf16[128,8320]{1,0:T(8,128)(2,1)S(1)}, bf16[128,8320]{1,0:T(8,128)(2,1)}, u32[]{:S(2)}) copy-start(bf16[128,8320]{1,0:T(8,128)(2,1)} %all-gather.4.cloned.1.call-done.same_ref) | copy-start | bytes 6389764
Sparse Core Ops, SparseCore 0:
  16.8 43.1 all-gather.3

commit v2 on v1

--- a/solution.py
+++ b/solution.py
@@ -87,11 +87,11 @@
             [
                 lax.dot_general(
                     coef,
-                    part[:, pl.ds(base, WIN)],
+                    part[:rows, pl.ds(base, WIN)],
                     (((1,), (1,)), ((), ())),
                     preferred_element_type=F32,
                 )
-                for part in (same_ref, near_ref, far_ref)
+                for part, rows in ((same_ref, 128), (near_ref, 64), (far_ref, 64))
             ],
             1,
         )
@@ -135,7 +135,7 @@
     return jnp.where(low, pltpu.roll(first, 64, 1), second)
 
 
-def waves_kernel(source_ref, table_ref, after_ref, out_ref):
+def waves_kernel(source_ref, table_ref, out_ref):
     column = lax.broadcasted_iota(jnp.int32, (2 * L, 2 * L), 1)
     chosen = jnp.where(column == source_ref[...], 1.0, 0.0).astype(BF16)
     step = 512
@@ -145,18 +145,18 @@
         ).astype(BF16)
 
 
-def wave_rows(source, table, after):
+def wave_rows(source, table):
     return pl.pallas_call(
         waves_kernel,
         out_shape=jax.ShapeDtypeStruct((2 * L, NPHI), BF16),
-        in_specs=[vmem(), vmem(), anywhere()],
+        in_specs=[vmem(), vmem()],
         out_specs=vmem(),
         compiler_params=params(),
         cost_estimate=pl.CostEstimate(
             flops=8 * L * L * NPHI, bytes_accessed=8 * L * NPHI, transcendentals=0
         ),
         name="waves",
-    )(source, table, after)
+    )(source, table)
 
 
 def azimuth_kernel(g_ref, t_ref, row_ref, lane_ref, out_ref, a_ref, h_ref):
@@ -244,7 +244,7 @@
         rows_b = turned_b[pl.ds(s, 32, stride=32), :].astype(BF16)
         window = pl.ds(base, WIN)
         both = jnp.dot(rows_a, same_ref[:, window], preferred_element_type=F32)
-        rest = jnp.concatenate([near_ref[:, window], far_ref[:, window]], 0)
+        rest = jnp.concatenate([near_ref[:64, window], far_ref[:64, window]], 0)
         both += jnp.dot(rows_b, rest, preferred_element_type=F32)
         merged = both[:16] + jnp.where(even, both[16:], -both[16:])
         held = out[:, pl.ds(base, WIN)]
@@ -294,38 +294,36 @@
     )(legendre)
 
 
-def hold_kernel(x_ref, after_ref, out_ref):
-    out_ref[...] = x_ref[...]
-
-
-def hold(x, after):
+def hold_kernel(x_ref, *refs):
+    refs[-1][...] = x_ref[...]
+
+
+def hold(x, *after):
     return pl.pallas_call(
         hold_kernel,
         out_shape=jax.ShapeDtypeStruct(x.shape, x.dtype),
-        in_specs=[vmem(), anywhere()],
+        in_specs=[vmem()] + [anywhere()] * len(after),
         out_specs=vmem(),
         compiler_params=params(),
         name="hold",
-    )(x, after)
-
-
-def gathered_table(legendre):
+    )(x, *after)
+
+
+def gathered_table(legendre, magnetic, *before):
     padded, legendre = entry(legendre)
     same = lax.all_gather(padded, ("y", "c"), axis=0, tiled=True)
     other = lax.ppermute(legendre, "xl", [(0, 1), (1, 0)])
-    near = lax.all_gather(other, "y", axis=0)
-    near = jnp.pad(near, ((0, 0), (0, 2), (0, 0))).reshape(64, PACK)
+    near = jnp.concatenate([lax.all_gather(hold(other, *before), "y", axis=0), magnetic[None]], 0)
+    near = jnp.pad(near, ((0, 0), (0, 2), (0, 0))).reshape(72, PACK)
     far = lax.ppermute(near, "c", [(0, 1), (1, 0)])
     return same, near, far
 
 
-def radial_slope(magnetic, after):
+def radial_slope(magnetic, far, *after):
     count = lax.axis_size(RAD)
     links = [(i, i + 1) for i in range(1, count - 1, 2)]
-    magnetic = hold(magnetic, after)
-    swapped = lax.ppermute(magnetic, "c", [(0, 1), (1, 0)])
-    linked = lax.ppermute(magnetic, RAD, links + [(j, i) for i, j in links])
-    swapped, linked = swapped.astype(F32), linked.astype(F32)
+    linked = lax.ppermute(hold(magnetic, *after), RAD, links + [(j, i) for i, j in links])
+    swapped, linked = far[64:70].astype(F32), linked.astype(F32)
     first = lax.axis_index("c") == 0
     slope = jnp.where(first, swapped - linked, linked - swapped)
     return (slope * 0.5).astype(BF16)
@@ -350,17 +348,16 @@
     ord_index = lax.axis_index(ORD)
     local_orders = lax.dynamic_slice_in_dim(orders, ord_index * SLOTS, SLOTS)
     lengths = L - local_orders
-    same, near, far = gathered_table(legendre)
-    slope = radial_slope(magnetic, near)
-    spec = jnp.concatenate([velocity, magnetic, slope, jnp.zeros_like(velocity)], 0)
-
     swapped = jnp.transpose(orders.reshape(8, 2, SLOTS), (1, 0, 2)).reshape(L)
     source = swapped.reshape(16, 1, SLOTS) + jnp.array([0, L], jnp.int32)[None, :, None]
     unscale = jnp.where(swapped == 0, 1.0, 0.5).astype(F32).reshape(16, 1, SLOTS)
     lane_scale = jnp.broadcast_to(unscale, (16, 2, SLOTS)).reshape(1, 2 * L)
     row_scale = table_weights(quad_weights) * (NPHI ** (-0.5))
+    waves = wave_rows(source.reshape(2 * L, 1), jnp.asarray(canonical_table()))
+    same, near, far = gathered_table(legendre, magnetic, waves, row_scale, lane_scale)
+    slope = radial_slope(magnetic, far, near)
+    spec = jnp.concatenate([velocity, magnetic, slope, jnp.zeros_like(velocity)], 0)
     grid = synthesis(offsets, lengths, spec, same, near, far)
-    waves = wave_rows(source.reshape(2 * L, 1), jnp.asarray(canonical_table()), grid)
     grid = lax.all_to_all(grid, SWAP, 0, 0)
     harmonic = azimuth(grid, waves, row_scale, lane_scale)
     spectra = lax.all_to_all(harmonic, SWAP, 0, 0)

time: 127 us -> 163 us (1.28)
  the two profiles are of different devices: /device:TPU:2 before, /device:TPU:24 now
where the time goes in v2:
time: 163 us; the launch traced here: 162 us
  blocking collectives  70.4 us (43%)
  waiting for transfers between devices  41.2 us (25%)
  Pallas kernels  15.7 us (10%)
  between operations  14.2 us (9%)
  starting transfers between devices  9.26 us (6%)
  local copies, waits for them, and re-layouts  9.2 us (6%)
  other arithmetic  2.35 us (1%)
    all_gather x1, waiting for transfers between devices, gathered_table(): same = lax.all_gather(padded, ('y', 'c'), axis=0, tiled=True)  39.3 us
    all_gather x1, blocking collectives, gathered_table(): lax.all_gather(hold(other, *before), 'y', axis=0)  27.1 us
    all_to_all x1, blocking collectives, shards(): grid = lax.all_to_all(grid, SWAP, 0, 0)  26.4 us
    all_to_all x1, blocking collectives, shards(): spectra = lax.all_to_all(harmonic, SWAP, 0, 0)  16.9 us
    unnamed x20, local copies, waits for them, and re-layouts  6.82 us
    pallas_call x1, Pallas kernels, synthesis(): pl.pallas_call(synthesis_kernel, out_shape=jax.ShapeDtypeStruct((16, ROWS...  5.82 us
    ppermute x1, starting transfers between devices, radial_slope(): lax.ppermute(hold(magnetic, *after), RAD, links + [(j, i) for i, j in lin...  3.78 us
    pallas_call x1, Pallas kernels, analysis(): pl.pallas_call(analysis_kernel, out_shape=(shape, shape), in_specs=[smem(...  3.47 us
  transfers between devices with their start and end apart: 4, of which 2 were waited for; matrix products, arithmetic and copies ran while one was open for 3% of the time, Pallas kernels for 2%

profile of v2, /device:TPU:24, one launch (start us, length us, event | category | flops | bytes accessed | tf_op | source)
XLA Modules:
  0.0 162.3 jit_solution(3475886231392637967)
XLA Ops:
  7.2 0.0 all-gather.4.cloned.1.call-start
  7.2 0.0 copy-start.6
  7.2 0.9 copy-done.6
  8.1 0.7 entry.1
  8.8 3.4 %collective-permute-start = (bf16[6,8320]{1,0:T(8,128)(2,1)S(1)}, bf16[6,8320]{1,0:T(8,128)(2,1)S(1)}, u32[]{:S(2)}, u32[]{:S(2)}) collective-permute-start(bf16[6,8320]{1,0:T(8,128)(2,1)S(1)} %get-tuple-element.6), channel_id=1, source_target_pairs={{0,256},{256,0},{1,257},{257,1},{2,258},{258,2},{3,259},{259,3},{4... | collective-permute-start | bytes 299528 | tf_op jit(solution)/shard_map/ppermute | solution.py:315
  12.2 0.8 reshape.105
  13.0 0.1 broadcast_add_fusion
  13.1 1.3 add.101.source_ref
  14.4 0.9 select_reduce_fusion
  15.3 0.0 copy-start.5
  15.3 1.0 copy-done.5
  16.4 0.0 copy-start.8
  16.4 1.9 %copy-done.8 = bf16[1024,1536]{1,0:T(8,128)(2,1)S(1)} copy-done((bf16[1024,1536]{1,0:T(8,128)(2,1)S(1)}, bf16[1024,1536]{1,0:T(8,128)(2,1)}, u32[]{:S(2)}) %copy-start.8) | copy-done | bytes 3145752
  18.2 3.5 %waves.1.refs_0_.t_ref = bf16[1024,1536]{1,0:T(8,128)(2,1)S(1)} custom-call(s32[1024,1]{1,0:T(8,128)S(1)} %copy-done.5, bf16[1024,1536]{1,0:T(8,128)(2,1)S(1)} %copy-done.8), custom_call_target="tpu_custom_call" | custom-call | flops 3221225472 | bytes 6291456 | tf_op jit(solution)/shard_map/waves/pallas_call | solution.py:149
  21.7 0.0 copy-start
  21.7 0.1 reshape.106.refs_2_.lane_ref
  21.8 0.1 copy.23.refs_1_.row_ref
  22.0 0.0 collective-permute-done.x_ref
  22.0 1.4 copy-done
  23.4 0.0 copy-start.4
  23.4 27.1 %all-gather.1 = bf16[8,6,8320]{2,1,0:T(8,128)(2,1)S(1)} all-gather(bf16[1,6,8320]{2,1,0:T(8,128)(2,1)S(1)} %bitcast.18), channel_id=2, replica_groups=mesh['xl'=2,'y'=8,'c'=2,'z'=8,'xh'=2] {'y'}, dimensions={0}, use_global_device_ids=true | all-gather | bytes 898560 | tf_op jit(solution)/shard_map/all_gather | solution.py:316
  50.5 0.0 copy-done.4
  50.5 0.4 fusion.3.refs_0_.near_ref
  50.8 0.0 copy-start.9
  50.8 2.1 %collective-permute-start.1 = (bf16[72,8320]{1,0:T(8,128)(2,1)S(1)}, bf16[72,8320]{1,0:T(8,128)(2,1)S(1)}, u32[]{:S(2)}, u32[]{:S(2)}) collective-permute-start(bf16[72,8320]{1,0:T(8,128)(2,1)S(1)} %fusion.3.refs_0_.near_ref), channel_id=1, source_target_pairs={{0,16},{16,0},{1,17},{17,1},{2,18},{18,2},{3,19},{19,3},{4,20},{20... | collective-permute-start | bytes 3594248 | tf_op jit(solution)/shard_map/ppermute | solution.py:318
  52.9 0.0 all-gather.4.cloned.1.call-update
  53.0 0.1 pad.8.clone
  53.0 0.0 copy-start.7
  53.0 3.8 %collective-permute-start.2 = (bf16[6,8320]{1,0:T(8,128)(2,1)S(1)}, bf16[6,8320]{1,0:T(8,128)(2,1)S(1)}, u32[]{:S(2)}, u32[]{:S(2)}) collective-permute-start(bf16[6,8320]{1,0:T(8,128)(2,1)S(1)} %hold.3), channel_id=1, source_target_pairs={{16,32},{48,64},{80,96},{112,128},{144,160},{176,192},{208,224},{2... | collective-permute-start | bytes 299528 | tf_op jit(solution)/shard_map/ppermute | solution.py:325
  56.8 0.8 dynamic-slice_subtract_fusion.len_ref
  57.6 1.9 %collective-permute-done.2 = bf16[6,8320]{1,0:T(8,128)(2,1)S(1)} collective-permute-done((bf16[6,8320]{1,0:T(8,128)(2,1)S(1)}, bf16[6,8320]{1,0:T(8,128)(2,1)S(1)}, u32[]{:S(2)}, u32[]{:S(2)}) %collective-permute-start.2) | collective-permute-done | bytes 99872 | tf_op jit(solution)/shard_map/ppermute | solution.py:325
  59.5 0.0 collective-permute-done.1.far_ref
  59.5 0.1 fusion.6
  59.6 0.0 copy-done.9
  59.6 0.2 maximum_maximum_fusion.spec_ref
  59.8 39.3 %all-gather.4.cloned.1.call-done.same_ref = bf16[128,8320]{1,0:T(8,128)(2,1)} async-done(((bf16[8,8320]{1,0:T(8,128)(2,1)}), bf16[128,8320]{1,0:T(8,128)(2,1)}) %all-gather.4.cloned.1.call-update) | async-done | bytes 2129936 | tf_op jit(solution)/shard_map/all_gather | solution.py:314
  99.1 0.0 copy-done.7
  99.1 0.0 copy-start.2
  99.1 1.6 copy-done.2
  100.7 0.0 copy-start.1
  100.7 5.8 %synthesis.1 = bf16[16,24,640]{2,1,0:T(8,128)(2,1)S(1)} custom-call(s32[32]{0:T(128)S(1)} %copy-done.7, s32[32]{0:T(128)S(1)} %dynamic-slice_subtract_fusion.len_ref, bf16[24,8320]{1,0:T(8,128)(2,1)S(1)} %maximum_maximum_fusion.spec_ref, bf16[128,8320]{1,0:T(8,128)(2,1)S(1)} %copy-done.2, bf16[72,8320]{1,0:T(8,128)(2,1)S(1)} %fusion.3.refs_0_.near_ref, ...), custom_call_target="tpu_custom_call" | custom-call | tf_op jit(solution)/shard_map/synthesis/pallas_call | solution.py:116
  106.5 26.4 %all_to_all.10.g_ref = bf16[16,24,640]{2,1,0:T(8,128)(2,1)S(1)} all-to-all(bf16[16,24,640]{2,1,0:T(8,128)(2,1)S(1)} %synthesis.1), channel_id=1, replica_groups=mesh['xl'=2,'y'=8,'c'=2,'z'=8,'xh'=2] {'xh','z'}, dimensions={0} | all-to-all | bytes 983040 | tf_op jit(solution)/shard_map/all_to_all | solution.py:361
  132.9 0.0 copy-done.1
  132.9 0.0 copy-start.3
  132.9 2.2 %azimuth.1 = bf16[16,24,384]{2,1,0:T(8,128)(2,1)S(1)} custom-call(bf16[16,24,640]{2,1,0:T(8,128)(2,1)S(1)} %all_to_all.10.g_ref, bf16[1024,1536]{1,0:T(8,128)(2,1)S(1)} %copy-done.1, f32[144,1]{1,0:T(8,128)S(1)} %copy.23.refs_1_.row_ref, f32[1,1024]{1,0:T(1,128)S(1)} %reshape.106.refs_2_.lane_ref), custom_call_target="tpu_custom_call" | custom-call | tf_op jit(solution)/shard_map/azimuth/pallas_call | solution.py:209
  135.1 16.9 %all_to_all.11.r_ref = bf16[16,24,384]{2,1,0:T(8,128)(2,1)S(1)} all-to-all(bf16[16,24,384]{2,1,0:T(8,128)(2,1)S(1)} %azimuth.1), channel_id=1, replica_groups=mesh['xl'=2,'y'=8,'c'=2,'z'=8,'xh'=2] {'xh','z'}, dimensions={0} | all-to-all | bytes 589824 | tf_op jit(solution)/shard_map/all_to_all | solution.py:363
  152.0 0.0 copy-done.3
  152.0 3.5 %analysis.1 = (bf16[6,8320]{1,0:T(8,128)(2,1)}, bf16[6,8320]{1,0:T(8,128)(2,1)}) custom-call(s32[32]{0:T(128)S(1)} %copy-done.7, s32[32]{0:T(128)S(1)} %dynamic-slice_subtract_fusion.len_ref, bf16[16,24,384]{2,1,0:T(8,128)(2,1)S(1)} %all_to_all.11.r_ref, bf16[128,8320]{1,0:T(8,128)(2,1)S(1)} %copy-done.3, bf16[72,8320]{1,0:T(8,128)(2,1)S(1)} %fusion.3.refs_0_.near_ref, ...), custom_call_target="tpu_custom_call" | custom-call | tf_op jit(solution)/shard_map/analysis/pallas_call | solution.py:261
  (9 shorter events, 0.1 us)
Async XLA Ops:
  7.2 91.9 %all-gather.4.cloned.1.call-start = ((), (), s32[]{:S(2)}) async-start(), calls=%async_computation.2 | async-start | bytes 2263040 | tf_op jit(solution)/shard_map/all_gather | solution.py:314
  7.2 0.9 copy-start.6
  8.8 13.2 %collective-permute-start = (bf16[6,8320]{1,0:T(8,128)(2,1)S(1)}, bf16[6,8320]{1,0:T(8,128)(2,1)S(1)}, u32[]{:S(2)}, u32[]{:S(2)}) collective-permute-start(bf16[6,8320]{1,0:T(8,128)(2,1)S(1)} %get-tuple-element.6), channel_id=1, source_target_pairs={{0,256},{256,0},{1,257},{257,1},{2,258},{258,2},{3,259},{259,3},{4... | collective-permute-start | bytes 299528 | tf_op jit(solution)/shard_map/ppermute | solution.py:315
  15.3 1.1 copy-start.5
  16.4 1.9 %copy-start.8 = (bf16[1024,1536]{1,0:T(8,128)(2,1)S(1)}, bf16[1024,1536]{1,0:T(8,128)(2,1)}, u32[]{:S(2)}) copy-start(bf16[1024,1536]{1,0:T(8,128)(2,1)} %constant.78.clone.table_ref) | copy-start | bytes 9437188
  21.7 1.6 %copy-start = (bf16[1024,1536]{1,0:T(8,128)(2,1)}, bf16[1024,1536]{1,0:T(8,128)(2,1)S(1)}, u32[]{:S(2)}) copy-start(bf16[1024,1536]{1,0:T(8,128)(2,1)S(1)} %waves.1.refs_0_.t_ref) | copy-start | bytes 9437188
  23.4 27.1 %copy-start.4 = (bf16[6,1,8320]{2,0,1:T(8,128)(2,1)S(1)}, bf16[6,1,8320]{2,0,1:T(8,128)(2,1)}, u32[]{:S(2)}) copy-start(bf16[6,1,8320]{2,0,1:T(8,128)(2,1)} %param.9) | copy-start | bytes 299524
  50.8 8.7 %copy-start.9 = (bf16[6,1,8320]{2,0,1:T(8,128)(2,1)S(1)}, bf16[6,1,8320]{2,0,1:T(8,128)(2,1)}, u32[]{:S(2)}) copy-start(bf16[6,1,8320]{2,0,1:T(8,128)(2,1)} %param.8) | copy-start | bytes 299524
  50.8 8.7 %collective-permute-start.1 = (bf16[72,8320]{1,0:T(8,128)(2,1)S(1)}, bf16[72,8320]{1,0:T(8,128)(2,1)S(1)}, u32[]{:S(2)}, u32[]{:S(2)}) collective-permute-start(bf16[72,8320]{1,0:T(8,128)(2,1)S(1)} %fusion.3.refs_0_.near_ref), channel_id=1, source_target_pairs={{0,16},{16,0},{1,17},{17,1},{2,18},{18,2},{3,19},{19,3},{4,20},{20... | collective-permute-start | bytes 3594248 | tf_op jit(solution)/shard_map/ppermute | solution.py:318
  53.0 46.0 %copy-start.7 = (s32[32]{0:T(128)S(1)}, s32[32]{0:T(128)}, u32[]{:S(2)}) copy-start(s32[32]{0:T(128)} %off_ref.3) | copy-start | bytes 388
  53.0 6.4 %collective-permute-start.2 = (bf16[6,8320]{1,0:T(8,128)(2,1)S(1)}, bf16[6,8320]{1,0:T(8,128)(2,1)S(1)}, u32[]{:S(2)}, u32[]{:S(2)}) collective-permute-start(bf16[6,8320]{1,0:T(8,128)(2,1)S(1)} %hold.3), channel_id=1, source_target_pairs={{16,32},{48,64},{80,96},{112,128},{144,160},{176,192},{208,224},{2... | collective-permute-start | bytes 299528 | tf_op jit(solution)/shard_map/ppermute | solution.py:325
  99.1 1.6 copy-start.2
  100.7 32.2 %copy-start.1 = (bf16[1024,1536]{1,0:T(8,128)(2,1)S(1)}, bf16[1024,1536]{1,0:T(8,128)(2,1)}, u32[]{:S(2)}) copy-start(bf16[1024,1536]{1,0:T(8,128)(2,1)} %copy-done) | copy-start | bytes 9437188
  132.9 19.1 %copy-start.3 = (bf16[128,8320]{1,0:T(8,128)(2,1)S(1)}, bf16[128,8320]{1,0:T(8,128)(2,1)}, u32[]{:S(2)}) copy-start(bf16[128,8320]{1,0:T(8,128)(2,1)} %all-gather.4.cloned.1.call-done.same_ref) | copy-start | bytes 6389764
Sparse Core Ops, SparseCore 0:
  53.0 45.9 all-gather.3
